TPU v7x, 256 devices: a whole 4x4x8 slice. The times are simulated.
256 devices in a mesh: group: 8 (over x, y_lo), blk: 32 (over z, y_hi, core).
Axes of the slice: x: 4, y: 4 (y_hi: 2, y_lo: 2; y = y_hi * 2 + y_lo), z: 8, core: 2. Of those that a mesh axis runs over, the one named last changes fastest.
Arguments:
- img_feat: bfloat16 [131072, 1152], P(('group', 'blk')), may hold values from -6 to 6
- txt_feat: bfloat16 [131072, 1152], P(('group', 'blk')), may hold values from -6 to 6
- img_proj: bfloat16 [1152, 1152], replicated, may hold values from -0.1875 to 0.1875
- txt_proj: bfloat16 [1152, 1152], replicated, may hold values from -0.1875 to 0.1875
- pos_index: int32 [131072], P(('group', 'blk')), may hold values from 0 to 16383, as said below
- logit_scale: float32 [1], replicated, may hold values from 10 to 40
- logit_bias: float32 [1], replicated, may hold values from -3 to 0
Outputs:
- img_feat_grad: bfloat16 [131072, 1152], P(('group', 'blk'))
- txt_feat_grad: bfloat16 [131072, 1152], P(('group', 'blk'))
- img_proj_grad: float32 [1152, 1152], P('blk')
- txt_proj_grad: float32 [1152, 1152], P('blk')
Inputs may be any that keep to these rules, and one draw needn't show every extreme that they name: `pos_index`: the matching text row of an image row in block k lies in block (k - o) mod (32) for some o in 0 .. 2; several image rows may match one text row.
All inputs are finite; a program needn't handle non-finite values.
Results may differ from a plain program's by a relative error of at most 0.018.
Values may be sent and summed in bfloat16 or wider, within the bound.
A program may use at most 64 MiB of HBM per device.

v0:
```python
import jax
import jax.numpy as jnp
from jax import lax
from jax.sharding import PartitionSpec as P

STEPS = 3


epsilon = 1e-06


def shifted(value, axis, steps):
    count = lax.axis_size(axis)
    pairs = [(source, (source + steps) % count) for source in range(count)]
    return lax.ppermute(value, axis, pairs)


def unit_rows(features, projection):
    embedded = jnp.dot(features, projection, preferred_element_type=jnp.float32)
    inverse = lax.rsqrt(jnp.sum(embedded * embedded, axis=-1, keepdims=True) + epsilon)
    exact = embedded * inverse
    return (exact.astype(jnp.bfloat16), exact, inverse)


def norm_backward(exact, inverse, upstream):
    return inverse * (upstream - exact * jnp.sum(exact * upstream, axis=-1, keepdims=True))


def transposed(left, right):
    return lax.dot_general(
        left, right, (((0,), (0,)), ((), ())), preferred_element_type=jnp.float32
    )


def against(left, right):
    return lax.dot_general(
        left, right, (((1,), (1,)), ((), ())), preferred_element_type=jnp.float32
    )


def per_device(img_feat, txt_feat, img_proj, txt_proj, pos_index, logit_scale, logit_bias):
    row_count = img_feat.shape[0]
    width = img_feat.shape[1]
    cycle_size = lax.axis_size("blk")
    my_block = lax.axis_index("blk")
    scale = logit_scale[0]
    bias = logit_bias[0]
    img_unit, img_exact, img_inverse = unit_rows(img_feat, img_proj)
    txt_unit, txt_exact, txt_inverse = unit_rows(txt_feat, txt_proj)
    columns = jnp.arange(row_count, dtype=jnp.int32)
    img_grad = jnp.zeros((row_count, width), jnp.float32)
    carried = jnp.zeros((row_count, width), jnp.float32)
    visiting = txt_unit
    for offset in range(STEPS):
        if offset > 0:
            visiting = shifted(visiting, "blk", 1)
        owner = (my_block - offset) % cycle_size
        matches = pos_index[:, None] == owner * row_count + columns[None, :]
        logits = scale * against(img_unit, visiting) + bias
        weights = (jax.nn.sigmoid(logits) - matches.astype(jnp.float32)).astype(jnp.bfloat16)
        img_grad = img_grad + scale * jnp.dot(weights, visiting, preferred_element_type=jnp.float32)
        shares = scale * transposed(weights, img_unit)
        carried = carried + shares
        if offset + 1 < STEPS:
            carried = shifted(carried.astype(jnp.bfloat16), "blk", 1).astype(carried.dtype)
    txt_grad = shifted(carried.astype(jnp.bfloat16), "blk", 1 - STEPS).astype(carried.dtype)
    img_delta = norm_backward(img_exact, img_inverse, img_grad).astype(jnp.bfloat16)
    txt_delta = norm_backward(txt_exact, txt_inverse, txt_grad).astype(jnp.bfloat16)
    img_back = against(img_delta, img_proj).astype(jnp.bfloat16)
    txt_back = against(txt_delta, txt_proj).astype(jnp.bfloat16)
    img_part = transposed(img_feat, img_delta)
    txt_part = transposed(txt_feat, txt_delta)
    summed = lax.psum_scatter(
        jnp.concatenate([img_part, txt_part], axis=1).astype(jnp.bfloat16),
        "blk",
        scatter_dimension=0,
        tiled=True,
    ).astype(jnp.float32)
    summed = lax.psum(summed.astype(jnp.bfloat16), "group").astype(jnp.float32)
    return (img_back, txt_back, summed[:, :width], summed[:, width:])


def solution(mesh):
    in_specs = (
        P(("group", "blk"), None),
        P(("group", "blk"), None),
        P(),
        P(),
        P(("group", "blk")),
        P(),
        P(),
    )
    out_specs = (
        P(("group", "blk"), None),
        P(("group", "blk"), None),
        P("blk", None),
        P("blk", None),
    )
    return jax.shard_map(
        per_device, mesh=mesh, in_specs=in_specs, out_specs=out_specs, check_vma=False
    )
```

profile of v0, /device:TPU:1, one launch (start us, length us, event | category | flops | bytes accessed | tf_op | source)
XLA Modules:
  0.0 483.4 jit_solution(3375525709205488298)
XLA Ops:
  7.2 4.2 multiply_reduce_fusion.1
  14.1 4.3 collective-permute-start
  18.4 4.5 multiply_reduce_fusion.2
  26.1 2.8 fusion.25
  28.9 1.9 fusion.3
  30.8 2.2 fusion.29
  33.0 2.8 collective-permute-start.1
  35.8 2.4 fusion.26
  38.2 6.3 %collective-permute-done.2 = bf16[512,1152]{1,0:T(8,128)(2,1)} collective-permute-done((bf16[512,1152]{1,0:T(8,128)(2,1)}, bf16[512,1152]{1,0:T(8,128)(2,1)}, u32[]{:S(2)}, u32[]{:S(2)}) %collective-permute-start.2) | collective-permute-done | bytes 1179680 | tf_op jit(solution)/shard_map/ppermute | solution.py:15
  44.5 2.2 add_convert_fusion.1
  46.6 4.2 collective-permute-start.3
  50.9 2.1 convolution_add_fusion.1
  53.0 4.1 collective-permute-done.1
  59.1 10.6 %collective-permute-done.3 = bf16[512,1152]{1,0:T(8,128)(2,1)S(1)} collective-permute-done((bf16[512,1152]{1,0:T(8,128)(2,1)S(1)}, bf16[512,1152]{1,0:T(8,128)(2,1)S(1)}, u32[]{:S(2)}, u32[]{:S(2)}) %collective-permute-start.3) | collective-permute-done | bytes 1179680 | tf_op jit(solution)/shard_map/ppermute | solution.py:15
  69.9 4.8 collective-permute-start.4
  78.9 16.4 %collective-permute-done.4 = bf16[512,1152]{1,0:T(8,128)(2,1)S(1)} collective-permute-done((bf16[512,1152]{1,0:T(8,128)(2,1)S(1)}, bf16[512,1152]{1,0:T(8,128)(2,1)S(1)}, u32[]{:S(2)}, u32[]{:S(2)}) %collective-permute-start.4) | collective-permute-done | bytes 1179680 | tf_op jit(solution)/shard_map/ppermute | solution.py:15
  99.1 2.8 pad_maximum_fusion
  103.8 4.1 convolution_convert_fusion.3
  108.0 283.9 %all-reduce.6.cloned.1.call-done = bf16[1152,2304]{0,1:T(8,128)(2,1)} async-done(((bf16[1152,2304]{0,1:T(8,128)(2,1)}), bf16[1152,2304]{0,1:T(8,128)(2,1)}) %all-reduce.6.cloned.1.call-update) | async-done | bytes 5308432
  391.8 2.4 constant_dynamic-slice_fusion
  394.2 5.0 %convolution_convert_fusion.2 = bf16[512,1152]{1,0:T(8,128)(2,1)} fusion(bf16[512,1152]{1,0:T(8,128)(2,1)} %copy-done.7, bf16[1152,1152]{1,0:T(8,128)(2,1)} %param.10), kind=kOutput, calls=%fused_computation.12 | convolution fusion | flops 1359544320 | bytes 5013504 | tf_op jit(solution)/shard_map/dot_general | solution.py:36
  399.2 72.5 %all-reduce.4.cloned.1.call-done = bf16[36,2304]{0,1:T(8,128)(2,1)} async-done(((bf16[36,2304]{0,1:T(8,128)(2,1)}), bf16[36,2304]{0,1:T(8,128)(2,1)}) %all-reduce.4.cloned.1.call-update) | async-done | bytes 165904 | tf_op jit(solution)/shard_map/psum | solution.py:79
  471.7 2.0 fusion.28
  473.7 2.0 copy.13
  (48 shorter events, 16.9 us)
Async XLA Ops:
  7.2 11.2 %copy-start = (bf16[1152,1152]{1,0:T(8,128)(2,1)S(1)}, bf16[1152,1152]{1,0:T(8,128)(2,1)}, u32[]{:S(2)}) copy-start(bf16[1152,1152]{1,0:T(8,128)(2,1)} %param.9) | copy-start | bytes 7962628
  7.2 384.7 %all-reduce.6.cloned.1.call-start = ((), (), s32[]{:S(2)}) async-start(), calls=%async_computation.1 | async-start | bytes 10616832
  11.4 1.4 copy-start.1
  14.1 19.0 %collective-permute-start = (bf16[512,1152]{1,0:T(8,128)(2,1)}, bf16[512,1152]{1,0:T(8,128)(2,1)}, u32[]{:S(2)}, u32[]{:S(2)}) collective-permute-start(bf16[512,1152]{1,0:T(8,128)(2,1)} %multiply_convert_fusion.1), channel_id=1, source_target_pairs={{0,1},{1,2},{2,3},{3,4},{4,5},{5,6},{6,7},{7,8},{8,9},{9,10},{10,1... | collective-permute-start | bytes 3538952 | tf_op jit(solution)/shard_map/ppermute | solution.py:15
  22.9 3.2 copy-start.10
  26.1 2.8 copy-start.4
  30.8 13.7 %collective-permute-start.2 = (bf16[512,1152]{1,0:T(8,128)(2,1)}, bf16[512,1152]{1,0:T(8,128)(2,1)}, u32[]{:S(2)}, u32[]{:S(2)}) collective-permute-start(bf16[512,1152]{1,0:T(8,128)(2,1)} %fusion.3), channel_id=1, source_target_pairs={{0,1},{1,2},{2,3},{3,4},{4,5},{5,6},{6,7},{7,8},{8,9},{9,10},{10,1... | collective-permute-start | bytes 3538952 | tf_op jit(solution)/shard_map/ppermute | solution.py:15
  30.8 5.0 %copy-start.5 = (bf16[512,1152]{1,0:T(8,128)(2,1)S(1)}, bf16[512,1152]{1,0:T(8,128)(2,1)}, u32[]{:S(2)}) copy-start(bf16[512,1152]{1,0:T(8,128)(2,1)} %copy-done.4) | copy-start | bytes 3538948
  33.0 24.1 %collective-permute-start.1 = (bf16[512,1152]{1,0:T(8,128)(2,1)}, bf16[512,1152]{1,0:T(8,128)(2,1)S(1)}, u32[]{:S(2)}, u32[]{:S(2)}) collective-permute-start(bf16[512,1152]{1,0:T(8,128)(2,1)} %collective-permute-done), channel_id=1, source_target_pairs={{0,1},{1,2},{2,3},{3,4},{4,5},{5,6},{6,7},{7,8},{8,9},{9,10},{10,1... | collective-permute-start | bytes 3538952 | tf_op jit(solution)/shard_map/ppermute | solution.py:15
  46.6 23.0 %collective-permute-start.3 = (bf16[512,1152]{1,0:T(8,128)(2,1)S(1)}, bf16[512,1152]{1,0:T(8,128)(2,1)S(1)}, u32[]{:S(2)}, u32[]{:S(2)}) collective-permute-start(bf16[512,1152]{1,0:T(8,128)(2,1)S(1)} %add_convert_fusion.1), channel_id=1, source_target_pairs={{0,1},{1,2},{2,3},{3,4},{4,5},{5,6},{6,7},{7,8},{8,9},{9,10},{10,1... | collective-permute-start | bytes 3538952 | tf_op jit(solution)/shard_map/ppermute | solution.py:15
  59.1 15.7 %copy-start.3 = (f32[512,1152]{1,0:T(8,128)S(1)}, f32[512,1152]{1,0:T(8,128)}, u32[]{:S(2)}) copy-start(f32[512,1152]{1,0:T(8,128)} %get-tuple-element.15) | copy-start | bytes 7077892
  69.9 25.4 %collective-permute-start.4 = (bf16[512,1152]{1,0:T(8,128)(2,1)S(1)}, bf16[512,1152]{1,0:T(8,128)(2,1)S(1)}, u32[]{:S(2)}, u32[]{:S(2)}) collective-permute-start(bf16[512,1152]{1,0:T(8,128)(2,1)S(1)} %add_convert_fusion), channel_id=1, source_target_pairs={{0,30},{1,31},{2,0},{3,1},{4,2},{5,3},{6,4},{7,5},{8,6},{9,7},{10,... | collective-permute-start | bytes 3538952 | tf_op jit(solution)/shard_map/ppermute | solution.py:15
  75.9 1.3 copy-start.8
  77.2 1.8 copy-start.6
  77.2 18.2 %copy-start.2 = (f32[512,1152]{1,0:T(8,128)S(1)}, f32[512,1152]{1,0:T(8,128)}, u32[]{:S(2)}) copy-start(f32[512,1152]{1,0:T(8,128)} %copy-done.1) | copy-start | bytes 7077892
  95.8 1.6 copy-start.9
  96.3 1.0 copy-start.7
  101.9 0.7 copy-start.11
  101.9 369.8 %all-reduce.4.cloned.1.call-start = ((), (), s32[]{:S(2)}) async-start(), calls=%async_computation | async-start | bytes 1179648 | tf_op jit(solution)/shard_map/psum | solution.py:79
Sparse Core Ops, SparseCore 0:
  102.0 289.7 all-reduce.5
  394.7 77.0 all-reduce.3
where the time goes:
time: 488 us; the launch traced here: 483 us
  waiting for transfers between devices  394 us (81%)
  matrix products  38 us (8%)
  starting transfers between devices  16.4 us (3%)
  between operations  16.2 us (3%)
  local copies, waits for them, and re-layouts  11.5 us (2%)
  other arithmetic  7.55 us (2%)
    unnamed x3, waiting for transfers between devices  284 us
    psum x1, waiting for transfers between devices, per_device(): summed = lax.psum(summed.astype(jnp.bfloat16), 'group').astype(jnp.float32)  72.5 us
    ppermute x5, waiting for transfers between devices, shifted(): return lax.ppermute(value, axis, pairs)  37.3 us
    ppermute x5, starting transfers between devices, shifted(): return lax.ppermute(value, axis, pairs)  16.1 us
    dot_general x5, matrix products, against(): lax.dot_general(left, right, (((1,), (1,)), ((), ())), preferred_element_...  15.3 us
  transfers between devices with their start and end apart: 7, of which 6 were waited for; matrix products, arithmetic and copies ran while one was open for 7% of the time, Pallas kernels for 0%

commit v1 on v0

v1 whole, which is shorter than its diff:
```python
import functools

import jax
import jax.numpy as jnp
from jax import lax
from jax.experimental import pallas as pl
from jax.experimental.pallas import tpu as pltpu
from jax.sharding import PartitionSpec as P

MESH = pl.DeviceIdType.MESH
EPSILON = 1e-06
ROWS = 512
WIDTH = 1152
HALF = 256
MSG = 128
NMSG = ROWS // MSG
TILES = WIDTH // 128
CHUNKS = ((0, 2), (2, 2), (4, 2), (6, 2), (8, 1))
NCH = len(CHUNKS)
ZROWS = 144
WIN = 48
OUT_ROWS = 36
BF16 = jnp.bfloat16
F32 = jnp.float32


def against(left, right):
    return lax.dot_general(
        left, right, (((1,), (1,)), ((), ())), preferred_element_type=F32
    )


def kernel(
    img_feat_hbm, txt_feat_hbm, img_proj_hbm, txt_proj_hbm, pos_hbm, scale_ref, bias_ref,
    img_back_hbm, txt_back_hbm, img_out, txt_out,
    img_feat, txt_feat, img_proj, txt_proj, pos,
    img_own, txt_own, img_dir, txt_dir, img_side, txt_side, pos_dir, pos_side, pos_rows,
    img_exact, txt_exact, img_inv, txt_inv, img_grad, txt_grad, weights,
    img_turned, txt_turned, img_delta, txt_delta, img_back, txt_back,
    part, r1, ra, q2, rb, q3, rz, q4, fin,
    load_sem, store_sem,
    ts_send, ts_recv, td_send, td_recv, is_send, is_recv, id_send, id_recv, pos_send, pos_recv,
    rs_send, rs_recv, self_send,
):
    group = lax.axis_index("group")
    blk = lax.axis_index("blk")
    x, y_lo = group // 2, lax.rem(group, 2)
    z, y_hi, c = blk // 4, lax.rem(blk // 2, 2), lax.rem(blk, 2)
    y = 2 * y_hi + y_lo
    quarter = 2 * y_hi + c

    def device(x, y, z, c):
        return (x * 2 + lax.rem(y, 2), z * 4 + (y // 2) * 2 + c)

    following = (group, lax.rem(blk + 2, 32))
    previous = (group, lax.rem(blk + 30, 32))
    sibling = (group, blk + 1 - 2 * c)
    root_z = x + 4 * c
    is_root = z == root_z

    def x_peer(d):
        return lax.rem(x + d, 4)

    def y_peer(d):
        return lax.rem(y + d, 4)

    def load(index, src, dst):
        return pltpu.make_async_copy(src, dst, load_sem.at[index])

    loads = [
        load(0, txt_proj_hbm, txt_proj),
        load(1, txt_feat_hbm, txt_feat),
        load(2, img_proj_hbm, img_proj),
        load(3, img_feat_hbm, img_feat),
        load(4, pos_hbm, pos.at[pl.ds(0, 8)]),
    ]
    for item in loads:
        item.start()

    barrier = pltpu.get_barrier_semaphore()

    def greet(target):
        pl.semaphore_signal(barrier, inc=1, device_id=target, device_id_type=MESH)

    greet(following)
    greet(previous)
    greet(sibling)
    for d in range(1, 4):
        greet(device(x_peer(d), y, z, c))
        greet(device(x, y_peer(d), z, c))
    source_x, source_c = lax.rem(z, 4), z // 4
    has_source = (source_x != x) | (source_c != c) | (quarter != y)

    @pl.when(has_source)
    def _():
        greet(device(source_x, quarter, z, source_c))

    @pl.when(is_root)
    def _():
        for d in range(1, 8):
            greet(device(x, y, lax.rem(z + d, 8), c))

    own_target = c == lax.rem(y, 2)
    count = 9 + jnp.where(is_root, 8 - jnp.where(own_target, 1, 0), 1)

    scale = scale_ref[0]
    bias = bias_ref[0]

    def embed(feat, proj, exact, own, inv, start):
        for n in range(3):
            exact[pl.ds(start, HALF), pl.ds(n * 384, 384)] = jnp.dot(
                feat[pl.ds(start, HALF), :], proj[:, pl.ds(n * 384, 384)],
                preferred_element_type=F32,
            )

        def rows(i, _):
            at = pl.ds(pl.multiple_of(start + i * 64, 64), 64)
            value = exact[at, :]
            inverse = lax.rsqrt(jnp.sum(value * value, axis=-1, keepdims=True) + EPSILON)
            unit = value * inverse
            exact[at, :] = unit
            own[at, :] = unit.astype(BF16)
            inv[at, :] = inverse
            return 0

        lax.fori_loop(0, HALF // 64, rows, 0)

    def message(src, dst, send, recv, index, target):
        at = pl.ds(index * MSG, MSG)
        return pltpu.make_async_remote_copy(
            src.at[at], dst.at[at], send.at[index], recv.at[index],
            device_id=target, device_id_type=MESH,
        )

    def txt_direct(index):
        return message(txt_own, txt_dir, td_send, td_recv, index, following)

    def img_direct(index):
        return message(img_own, img_dir, id_send, id_recv, index, previous)

    def txt_aside(src, index):
        return message(src, txt_side, ts_send, ts_recv, index, sibling)

    def img_aside(src, index):
        return message(src, img_side, is_send, is_recv, index, sibling)

    loads[0].wait()
    loads[1].wait()
    embed(txt_feat, txt_proj, txt_exact, txt_own, txt_inv, 0)
    pl.semaphore_wait(barrier, count)
    for index in (0, 1):
        txt_direct(index).start()

    @pl.when(c == 0)
    def _():
        for index in (0, 1):
            txt_aside(txt_own, index).start()

    embed(txt_feat, txt_proj, txt_exact, txt_own, txt_inv, HALF)
    for index in (2, 3):
        txt_direct(index).start()

    @pl.when(c == 0)
    def _():
        for index in (2, 3):
            txt_aside(txt_own, index).start()

    loads[4].wait()
    pos_ahead = pltpu.make_async_remote_copy(
        pos, pos_dir, pos_send.at[0], pos_recv.at[0], device_id=previous, device_id_type=MESH
    )
    pos_ahead.start()

    def pos_aside(src):
        return pltpu.make_async_remote_copy(
            src, pos_side, pos_send.at[1], pos_recv.at[1], device_id=sibling, device_id_type=MESH
        )

    @pl.when(c == 1)
    def _():
        pos_aside(pos).start()

    loads[2].wait()
    loads[3].wait()
    embed(img_feat, img_proj, img_exact, img_own, img_inv, 0)
    embed(img_feat, img_proj, img_exact, img_own, img_inv, HALF)

    @pl.when(c == 1)
    def _():
        for index in range(NMSG):
            img_aside(img_own, index).start()

    for h in range(2):
        row = jnp.broadcast_to(pos[h : h + 1, :], (HALF, HALF))
        pos_rows[pl.ds(h * HALF, HALF), :] = row.T

    img_grad[...] = jnp.zeros_like(img_grad)
    txt_grad[...] = jnp.zeros_like(txt_grad)

    def turn(feat, turned):
        def step(t, _):
            at = pl.ds(pl.multiple_of(t * 128, 128), 128)
            turned[at, :] = feat[:, at].T
            return 0

        lax.fori_loop(0, TILES, step, 0)

    def pair(own, other, grad, matches, h):
        def block(m, _):
            at = pl.ds(pl.multiple_of(m * HALF, HALF), HALF)
            logits = scale * against(own[at, :], other[pl.ds(h * HALF, HALF), :]) + bias
            weight = jax.nn.sigmoid(logits) - matches(m, h).astype(F32)
            weights[at, :] = weight.astype(BF16)
            return 0

        lax.fori_loop(0, 2, block, 0)

        def columns(n, _):
            at = pl.ds(pl.multiple_of(n * 384, 384), 384)
            grad[:, at] += jnp.dot(
                weights[...], other[pl.ds(h * HALF, HALF), at], preferred_element_type=F32
            )
            return 0

        lax.fori_loop(0, 3, columns, 0)

    def txt_matches(back):
        owner = lax.rem(blk - back + 32, 32)

        def matches(m, h):
            first = owner * ROWS + h * HALF
            column = first + lax.broadcasted_iota(jnp.int32, (HALF, HALF), 1)
            return pos_rows[pl.ds(pl.multiple_of(m * HALF, HALF), HALF), :] == column

        return matches

    def img_matches(pos_ref):
        def matches(m, h):
            first = blk * ROWS + m * HALF
            row = first + lax.broadcasted_iota(jnp.int32, (HALF, HALF), 0)
            return jnp.broadcast_to(pos_ref[h : h + 1, :], (HALF, HALF)) == row

        return matches

    def pair_txt(other, back, h):
        pair(img_own, other, img_grad, txt_matches(back), h)

    def pair_img(other, pos_ref, h):
        pair(txt_own, other, txt_grad, img_matches(pos_ref), h)

    for h in range(2):
        pair_txt(txt_own, 0, h)
        pair_img(img_own, pos, h)

    pos_ahead.wait_recv()

    @pl.when(c == 0)
    def _():
        pos_aside(pos_dir).start()

    pos_aside(pos).wait_recv()

    def side_txt(h):
        for index in (2 * h, 2 * h + 1):
            txt_aside(txt_own, index).wait_recv()
        pair_txt(txt_side, 1, h)

    def side_img(h):
        for index in (2 * h, 2 * h + 1):
            img_aside(img_own, index).wait_recv()
        pair_img(img_side, pos_side, h)

    @pl.when(c == 1)
    def _():
        side_txt(0)
        side_txt(1)

    @pl.when(c == 0)
    def _():
        side_img(0)
        side_img(1)

    turn(img_feat, img_turned)
    turn(txt_feat, txt_turned)

    for h in range(2):
        for index in (2 * h, 2 * h + 1):
            txt_direct(index).wait_recv()

            @pl.when(c == 1)
            def _():
                txt_aside(txt_dir, index).start()

        if h == 1:
            for index in range(NMSG):
                txt_direct(index).wait_send()
            for index in range(NMSG):
                img_direct(index).start()
        pair_txt(txt_dir, 2, h)

        @pl.when(c == 0)
        def _():
            side_txt(h)

    def finish(grad, exact, inv, delta):
        def rows(i, _):
            at = pl.ds(pl.multiple_of(i * 64, 64), 64)
            value = scale * grad[at, :]
            unit = exact[at, :]
            along = jnp.sum(unit * value, axis=-1, keepdims=True)
            delta[at, :] = (inv[at, :] * (value - unit * along)).astype(BF16)
            return 0

        lax.fori_loop(0, ROWS // 64, rows, 0)

    def waiter(ref, sem):
        return pltpu.make_async_copy(ref, ref, sem)

    class Chunk:
        def __init__(self, u, ch):
            self.u, self.ch = u, ch
            first, count = CHUNKS[ch]
            self.t = pl.ds(first, count)
            self.first, self.count = first, count

        def sem(self, stage):
            return rs_send.at[self.u, self.ch, stage], rs_recv.at[self.u, self.ch, stage]

        def copy(self, stage, src, dst, target):
            send, recv = self.sem(stage)
            pltpu.make_async_remote_copy(
                src, dst, send, recv, device_id=target, device_id_type=MESH
            ).start()

        def make(self, turned, delta):
            def block(m, _):
                at = pl.ds(pl.multiple_of(m * 288, 288), 288)
                value = jnp.dot(
                    turned[at, :], delta[:, self.first * 128 : (self.first + self.count) * 128],
                    preferred_element_type=F32,
                ).astype(BF16)
                for i in range(self.count):
                    part[self.u, self.first + i, at, :] = value[:, i * 128 : (i + 1) * 128]
                return 0

            lax.fori_loop(0, 4, block, 0)
            other = pl.ds(pl.multiple_of(576 * (1 - c), 576), 576)
            self.copy(0, part.at[self.u, self.t, other], r1.at[self.u, self.t], sibling)

        def add_core(self):
            u, t = self.u, self.t
            send, recv = self.sem(0)
            waiter(r1.at[u, t], recv).wait()

            def step(i, _):
                tile = self.first + i
                mine = pl.ds(pl.multiple_of(576 * c, 576), 576)
                r1[u, tile] = (
                    part[u, tile, mine, :].astype(F32) + r1[u, tile].astype(F32)
                ).astype(BF16)
                return 0

            lax.fori_loop(0, self.count, step, 0)
            for d in range(1, 4):
                rows = pl.ds(pl.multiple_of(ZROWS * x_peer(d), ZROWS), ZROWS)
                self.copy(
                    1, r1.at[u, t, rows], ra.at[u, d - 1, t], device(x_peer(d), y, z, c)
                )

        def add_x(self):
            u, t = self.u, self.t
            waiter(ra.at[u, :, t], self.sem(1)[1]).wait()

            def step(i, _):
                tile = self.first + i
                rows = pl.ds(pl.multiple_of(ZROWS * x, ZROWS), ZROWS)
                total = r1[u, tile, rows, :].astype(F32)
                for d in range(3):
                    total = total + ra[u, d, tile].astype(F32)
                q2[u, tile] = total.astype(BF16)
                return 0

            lax.fori_loop(0, self.count, step, 0)
            for d in range(1, 4):
                rows = pl.ds(pl.multiple_of(32 * y_peer(d), 32), WIN)
                self.copy(
                    2, q2.at[u, t, rows], rb.at[u, d - 1, t], device(x, y_peer(d), z, c)
                )

        def add_y(self):
            u, t = self.u, self.t
            waiter(rb.at[u, :, t], self.sem(2)[1]).wait()

            def step(i, _):
                tile = self.first + i
                rows = pl.ds(pl.multiple_of(32 * y, 32), WIN)
                total = q2[u, tile, rows, :].astype(F32)
                for d in range(3):
                    total = total + rb[u, d, tile].astype(F32)
                q3[u, tile] = total.astype(BF16)
                return 0

            lax.fori_loop(0, self.count, step, 0)

            @pl.when(jnp.logical_not(is_root))
            def _():
                slot = lax.rem(z - root_z + 8, 8) - 1
                self.copy(3, q3.at[u, t], rz.at[u, slot, t], device(x, y, root_z, c))

        def targets(self):
            for dx in range(4):
                for dy in range(2):
                    far_y = 2 * y_hi + lax.rem(y_lo + dy, 2)
                    yield (dx, dy), device(x_peer(dx), far_y, z, y_lo)

        def add_z(self):
            u, t = self.u, self.t

            @pl.when(is_root)
            def _():
                waiter(rz.at[u, :, t], self.sem(3)[1]).wait()

                def step(i, _):
                    tile = self.first + i
                    total = q3[u, tile].astype(F32)
                    for d in range(7):
                        total = total + rz[u, d, tile].astype(F32)
                    q4[u, tile] = total.astype(BF16)
                    return 0

                lax.fori_loop(0, self.count, step, 0)
                for where, target in self.targets():
                    if where != (0, 0):
                        self.copy(4, q4.at[u, t], fin.at[u, t], target)
                    else:

                        @pl.when(own_target)
                        def _():
                            pltpu.make_async_copy(
                                q4.at[u, t], fin.at[u, t], self.sem(4)[1]
                            ).start()

                        @pl.when(jnp.logical_not(own_target))
                        def _():
                            pltpu.make_async_remote_copy(
                                q4.at[u, t], fin.at[u, t],
                                self_send.at[u, self.ch], self.sem(4)[1],
                                device_id=target, device_id_type=MESH,
                            ).start()

        def collect(self, out):
            u = self.u
            waiter(fin.at[u, self.t], self.sem(4)[1]).wait()
            for q in range(4):

                @pl.when(quarter == q)
                def _():
                    for i in range(self.count):
                        tile = self.first + i
                        out[:, tile * 128 : (tile + 1) * 128] = fin[u, tile].astype(F32)[
                            4 * q : 4 * q + OUT_ROWS
                        ]

        def drain(self):
            u, t = self.u, self.t
            waiter(r1.at[u, t], self.sem(0)[0]).wait()
            waiter(ra.at[u, :, t], self.sem(1)[0]).wait()
            waiter(rb.at[u, :, t], self.sem(2)[0]).wait()

            @pl.when(jnp.logical_not(is_root))
            def _():
                waiter(q3.at[u, t], self.sem(3)[0]).wait()

            @pl.when(is_root)
            def _():
                waiter(rz.at[u, :, t], self.sem(4)[0]).wait()

                @pl.when(jnp.logical_not(own_target))
                def _():
                    waiter(q4.at[u, t], self_send.at[u, self.ch]).wait()

    img_chunks = [Chunk(0, ch) for ch in range(NCH)]
    txt_chunks = [Chunk(1, ch) for ch in range(NCH)]

    def back(delta, proj, staged, out, index):
        def columns(n, _):
            at = pl.ds(pl.multiple_of(n * 384, 384), 384)
            staged[:, at] = against(delta[...], proj[at, :]).astype(BF16)
            return 0

        lax.fori_loop(0, 3, columns, 0)
        copy = pltpu.make_async_copy(staged, out, store_sem.at[index])
        copy.start()
        return copy

    finish(img_grad, img_exact, img_inv, img_delta)
    for chunk in img_chunks:
        chunk.make(img_turned, img_delta)
    for chunk in img_chunks:
        chunk.add_core()
    img_store = back(img_delta, img_proj, img_back, img_back_hbm, 0)

    for h in range(2):
        for index in (2 * h, 2 * h + 1):
            img_direct(index).wait_recv()

            @pl.when(c == 0)
            def _():
                img_aside(img_dir, index).start()

        pair_img(img_dir, pos_dir, h)

        @pl.when(c == 1)
        def _():
            side_img(h)

        if h == 0:
            for chunk in img_chunks[:2]:
                chunk.add_x()

    finish(txt_grad, txt_exact, txt_inv, txt_delta)
    for chunk in txt_chunks:
        chunk.make(txt_turned, txt_delta)
    for chunk in img_chunks[2:]:
        chunk.add_x()
    for chunk in txt_chunks:
        chunk.add_core()
    for chunk in img_chunks:
        chunk.add_y()
    for chunk in img_chunks:
        chunk.add_z()
    txt_store = back(txt_delta, txt_proj, txt_back, txt_back_hbm, 1)
    for chunk in txt_chunks:
        chunk.add_x()
    for chunk in txt_chunks:
        chunk.add_y()
    for chunk in txt_chunks:
        chunk.add_z()
    for chunk in img_chunks:
        chunk.collect(img_out)
    for chunk in txt_chunks:
        chunk.collect(txt_out)

    img_store.wait()
    txt_store.wait()
    for chunk in img_chunks + txt_chunks:
        chunk.drain()
    for index in range(NMSG):
        img_direct(index).wait_send()
        txt_aside(txt_own, index).wait_send()
        img_aside(img_own, index).wait_send()
    pos_ahead.wait_send()
    pos_aside(pos).wait_send()


def per_device(img_feat, txt_feat, img_proj, txt_proj, pos_index, logit_scale, logit_bias):
    pos = jnp.pad(pos_index.reshape(2, HALF), ((0, 6), (0, 0)))
    anywhere = pl.BlockSpec(memory_space=pl.ANY)
    scalar = pl.BlockSpec(memory_space=pltpu.SMEM)
    vmem = pl.BlockSpec(memory_space=pltpu.VMEM)
    block16 = pltpu.VMEM((ROWS, WIDTH), BF16)
    block32 = pltpu.VMEM((ROWS, WIDTH), F32)
    square = pltpu.VMEM((WIDTH, WIDTH), BF16)
    places = pltpu.VMEM((8, HALF), jnp.int32)
    dma = pltpu.SemaphoreType.DMA
    return pl.pallas_call(
        kernel,
        name="pairwise",
        out_shape=(
            jax.ShapeDtypeStruct((ROWS, WIDTH), BF16),
            jax.ShapeDtypeStruct((ROWS, WIDTH), BF16),
            jax.ShapeDtypeStruct((OUT_ROWS, WIDTH), F32),
            jax.ShapeDtypeStruct((OUT_ROWS, WIDTH), F32),
        ),
        in_specs=[anywhere] * 5 + [scalar] * 2,
        out_specs=(anywhere, anywhere, vmem, vmem),
        scratch_shapes=[
            block16, block16, square, square, places,
            block16, block16, block16, block16, block16, block16, places, places,
            pltpu.VMEM((ROWS, HALF), jnp.int32),
            block32, block32, pltpu.VMEM((ROWS, 1), F32), pltpu.VMEM((ROWS, 1), F32),
            block32, block32, pltpu.VMEM((ROWS, HALF), BF16),
            pltpu.VMEM((WIDTH, ROWS), BF16), pltpu.VMEM((WIDTH, ROWS), BF16),
            block16, block16, block16, block16,
            pltpu.VMEM((2, TILES, WIDTH, 128), BF16),
            pltpu.VMEM((2, TILES, WIDTH // 2, 128), BF16),
            pltpu.VMEM((2, 3, TILES, ZROWS, 128), BF16),
            pltpu.VMEM((2, TILES, ZROWS, 128), BF16),
            pltpu.VMEM((2, 3, TILES, WIN, 128), BF16),
            pltpu.VMEM((2, TILES, WIN, 128), BF16),
            pltpu.VMEM((2, 7, TILES, WIN, 128), BF16),
            pltpu.VMEM((2, TILES, WIN, 128), BF16),
            pltpu.VMEM((2, TILES, WIN, 128), BF16),
            dma((5,)), dma((2,)),
            dma((NMSG,)), dma((NMSG,)), dma((NMSG,)), dma((NMSG,)),
            dma((NMSG,)), dma((NMSG,)), dma((NMSG,)), dma((NMSG,)),
            dma((2,)), dma((2,)),
            dma((2, NCH, 5)), dma((2, NCH, 5)), dma((2, NCH)),
        ],
        compiler_params=pltpu.CompilerParams(
            collective_id=0, has_side_effects=True, vmem_limit_bytes=62 * 1024 * 1024
        ),
        cost_estimate=pl.CostEstimate(
            flops=15_000_000_000, bytes_accessed=12_000_000, transcendentals=1_500_000
        ),
    )(img_feat, txt_feat, img_proj, txt_proj, pos, logit_scale, logit_bias)


def solution(mesh):
    both = P(("group", "blk"), None)
    in_specs = (both, both, P(), P(), P(("group", "blk")), P(), P())
    out_specs = (both, both, P("blk", None), P("blk", None))
    return jax.shard_map(
        per_device, mesh=mesh, in_specs=in_specs, out_specs=out_specs, check_vma=False
    )
```

time: 488 us -> 122 us (0.25)
  waiting for transfers between devices: 394 us -> 0 us
  Pallas kernels: 0 us -> 113 us
  matrix products: 38 us -> 0 us
  starting transfers between devices: 16.4 us -> 0 us
  between operations: 16.2 us -> 1.95 us
  other arithmetic: 7.55 us -> 0 us
  local copies, waits for them, and re-layouts: 11.5 us -> 6.21 us
    unnamed x3 -> x0, waiting for transfers between devices: 284 us -> none
    pallas_call x0 -> x1, Pallas kernels: none -> 113 us  [per_device(): pl.pallas_call(kernel, name='pairwise', out_shape=(jax.ShapeDtypeStruct((...]
    psum x1 -> x0, waiting for transfers between devices: 72.5 us -> none  [per_device(): summed = lax.psum(summed.astype(jnp.bfloat16), 'group').astype(jnp.float32)]
    dot_general x15 -> x0, matrix products: 38 us -> none  [the longest x5 15.3 us: against(): lax.dot_general(left, right, (((1,), (1,)), ((), ())), preferred_element_...]
    ppermute x5 -> x0, waiting for transfers between devices: 37.3 us -> none  [shifted(): return lax.ppermute(value, axis, pairs)]
    ppermute x5 -> x0, starting transfers between devices: 16.1 us -> none  [shifted(): return lax.ppermute(value, axis, pairs)]
  transfers between devices with their start and end apart: 7 -> 0, of which waited for: 6 -> 0; matrix products, arithmetic and copies ran while one was open for 7% -> 0% of each run, Pallas kernels for 0% -> 0%
where the time goes in v1:
time: 122 us
  Pallas kernels  113 us (93%)
  local copies, waits for them, and re-layouts  6.21 us (5%)
  between operations  1.95 us (2%)
    pallas_call x1, Pallas kernels, per_device(): pl.pallas_call(kernel, name='pairwise', out_shape=(jax.ShapeDtypeStruct((...  113 us
    unnamed x10, local copies, waits for them, and re-layouts  4.91 us

profile of v1, /device:TPU:1, one launch (start us, length us, event | category | flops | bytes accessed | tf_op | source)
XLA Modules:
  0.0 121.6 jit_solution(8953996072999982777)
XLA Ops:
  1.9 0.7 reshape.11
  2.6 0.6 pad.4.pos_hbm
  3.2 113.5 %pairwise.1 = (bf16[512,1152]{1,0:T(8,128)(2,1)}, bf16[512,1152]{1,0:T(8,128)(2,1)}, f32[36,1152]{1,0:T(8,128)}, f32[36,1152]{1,0:T(8,128)}) custom-call(bf16[512,1152]{1,0:T(8,128)(2,1)} %img_feat_hbm.1, bf16[512,1152]{1,0:T(8,128)(2,1)} %txt_feat_hbm.1, bf16[1152,1152]{1,0:T(8,128)(2,1)} %img_proj_hbm.1, bf16[1152,1152]{1,0:T(8,128)(2,1)} %txt_proj_hbm.1, ...), custom_call_target="tpu_custom_call" | custom-call | flops 15000000512 | bytes 12000000 | tf_op jit(solution)/shard_map/pairwise/pallas_call | solution.py:566
  116.7 0.0 copy-start
  116.7 2.5 %copy.17 = bf16[512,1152]{1,0:T(8,128)(2,1)} copy(bf16[512,1152]{1,0:T(8,128)(2,1)} %get-tuple-element.8) | data formatting | bytes 2359296
  119.2 0.0 copy-done
  119.2 0.0 copy-start.2
  119.2 0.0 copy-start.1
  119.2 1.0 copy.18
  120.2 0.1 copy-done.2
  120.3 0.7 copy.19
  121.0 0.0 copy-done.1
  121.0 0.7 copy.20
Async XLA Ops:
  116.7 2.5 %copy-start = (bf16[512,1152]{1,0:T(8,128)(2,1)S(1)}, bf16[512,1152]{1,0:T(8,128)(2,1)}, u32[]{:S(2)}) copy-start(bf16[512,1152]{1,0:T(8,128)(2,1)} %get-tuple-element.9) | copy-start | bytes 3538948
  119.2 1.1 copy-start.2
  119.2 1.8 %copy-start.1 = (f32[36,1152]{1,0:T(8,128)S(1)}, f32[36,1152]{1,0:T(8,128)}, u32[]{:S(2)}) copy-start(f32[36,1152]{1,0:T(8,128)} %get-tuple-element.11) | copy-start | bytes 497668

commit v2 on v1

v2 whole, which is shorter than its diff:
```python
import functools

import jax
import jax.numpy as jnp
from jax import lax
from jax.experimental import pallas as pl
from jax.experimental.pallas import tpu as pltpu
from jax.sharding import PartitionSpec as P

MESH = pl.DeviceIdType.MESH
EPSILON = 1e-06
ROWS = 512
WIDTH = 1152
HALF = 256
STEP = 128
MSG = 64
NMSG = ROWS // MSG
PER_STEP = STEP // MSG
TILES = WIDTH // 128
CHUNKS = ((0, 2), (2, 2), (4, 2), (6, 2), (8, 1))
ORDERS = ("xxxxx", "xyxyx")
COLUMNS = tuple((n, min(256, WIDTH - n)) for n in range(0, WIDTH, 256))
NCH = len(CHUNKS)
ZROWS = 144
WIN = 48
OUT_ROWS = 36
BF16 = jnp.bfloat16
F32 = jnp.float32


def against(left, right):
    return lax.dot_general(
        left, right, (((1,), (1,)), ((), ())), preferred_element_type=F32
    )


def kernel(
    img_feat_hbm, txt_feat_hbm, img_proj_hbm, txt_proj_hbm, pos_hbm, scale_ref, bias_ref,
    img_back_hbm, txt_back_hbm, img_out, txt_out,
    img_feat, txt_feat, img_proj, txt_proj, pos,
    img_own, txt_own, img_dir, txt_dir, img_side, txt_side, pos_dir, pos_side, pos_rows,
    img_exact, txt_exact, img_inv, txt_inv, img_grad, txt_grad, weights,
    img_delta, txt_delta, img_back, txt_back,
    part, r1, ra, q2, rb, q3, rz, q4, fin,
    load_sem, store_sem,
    ts_send, ts_recv, td_send, td_recv, is_send, is_recv, id_send, id_recv, pos_send, pos_recv,
    rs_send, rs_recv, self_send, turn_sem,
):
    group = lax.axis_index("group")
    blk = lax.axis_index("blk")
    x, y_lo = group // 2, lax.rem(group, 2)
    z, y_hi, c = blk // 4, lax.rem(blk // 2, 2), lax.rem(blk, 2)
    y = 2 * y_hi + y_lo
    quarter = 2 * y_hi + c

    def device(x, y, z, c):
        return (x * 2 + lax.rem(y, 2), z * 4 + (y // 2) * 2 + c)

    following = (group, lax.rem(blk + 2, 32))
    previous = (group, lax.rem(blk + 30, 32))
    sibling = (group, blk + 1 - 2 * c)
    root_z = {"x": x + 4 * c, "y": y + 4 * c}
    is_root = {order: z == root_z[order] for order in "xy"}
    window = {"x": y, "y": x}
    own_target = {
        order: (y_hi == window[order] // 2) & (c == lax.rem(window[order], 2)) for order in "xy"
    }

    def x_peer(d):
        return lax.rem(x + d, 4)

    def y_peer(d):
        return lax.rem(y + d, 4)

    def load(index, src, dst):
        return pltpu.make_async_copy(src, dst, load_sem.at[index])

    loads = [
        load(0, txt_proj_hbm, txt_proj),
        load(1, txt_feat_hbm, txt_feat),
        load(2, img_proj_hbm, img_proj),
        load(3, img_feat_hbm, img_feat),
        load(4, pos_hbm, pos),
    ]
    for item in loads:
        item.start()

    barrier = pltpu.get_barrier_semaphore()

    def greet(target):
        pl.semaphore_signal(barrier, inc=1, device_id=target, device_id_type=MESH)

    greet(following)
    greet(previous)
    greet(sibling)
    for d in range(1, 4):
        greet(device(x_peer(d), y, z, c))
        greet(device(x, y_peer(d), z, c))
    sources = {
        "x": device(lax.rem(z, 4), quarter, z, z // 4),
        "y": device(quarter, lax.rem(z, 4), z, z // 4),
    }
    count = 9
    for order in "xy":
        source = sources[order]

        @pl.when((source[0] != group) | (source[1] != blk))
        def _():
            greet(source)

        @pl.when(is_root[order])
        def _():
            for d in range(1, 8):
                greet(device(x, y, lax.rem(z + d, 8), c))

        count = count + jnp.where(is_root[order], 8 - jnp.where(own_target[order], 1, 0), 1)

    scale = scale_ref[0]
    bias = bias_ref[0]

    def embed(feat, proj, exact, own, inv, start):
        for n, wide in COLUMNS:
            exact[start : start + STEP, n : n + wide] = jnp.dot(
                feat[start : start + STEP, :], proj[:, n : n + wide], preferred_element_type=F32
            )
        for i in range(STEP // 64):
            at = pl.ds(start + i * 64, 64)
            value = exact[at, :]
            inverse = lax.rsqrt(jnp.sum(value * value, axis=-1, keepdims=True) + EPSILON)
            unit = value * inverse
            exact[at, :] = unit
            own[at, :] = unit.astype(BF16)
            inv[at, :] = inverse

    def message(src, dst, send, recv, index, target):
        at = pl.ds(index * MSG, MSG)
        return pltpu.make_async_remote_copy(
            src.at[at], dst.at[at], send.at[index], recv.at[index],
            device_id=target, device_id_type=MESH,
        )

    def txt_direct(index):
        return message(txt_own, txt_dir, td_send, td_recv, index, following)

    def img_direct(index):
        return message(img_own, img_dir, id_send, id_recv, index, previous)

    def txt_aside(src, index):
        return message(src, txt_side, ts_send, ts_recv, index, sibling)

    def img_aside(src, index):
        return message(src, img_side, is_send, is_recv, index, sibling)

    loads[0].wait()
    loads[1].wait()
    for step in range(ROWS // STEP):
        embed(txt_feat, txt_proj, txt_exact, txt_own, txt_inv, step * STEP)
        if step == 0:
            pl.semaphore_wait(barrier, count)
        for index in range(step * PER_STEP, (step + 1) * PER_STEP):
            txt_direct(index).start()

            @pl.when(c == 0)
            def _():
                txt_aside(txt_own, index).start()

    loads[4].wait()
    pos_ahead = pltpu.make_async_remote_copy(
        pos, pos_dir, pos_send.at[0], pos_recv.at[0], device_id=previous, device_id_type=MESH
    )
    pos_ahead.start()

    def pos_aside(src):
        return pltpu.make_async_remote_copy(
            src, pos_side, pos_send.at[1], pos_recv.at[1], device_id=sibling, device_id_type=MESH
        )

    @pl.when(c == 1)
    def _():
        pos_aside(pos).start()

    loads[2].wait()
    loads[3].wait()
    for step in range(ROWS // STEP):
        embed(img_feat, img_proj, img_exact, img_own, img_inv, step * STEP)

    @pl.when(c == 1)
    def _():
        for index in range(NMSG):
            img_aside(img_own, index).start()

    def pos_row(pos_ref, first, many):
        return jnp.concatenate([pos_ref[first + i : first + i + 1, :] for i in range(many)], axis=1)

    for h in range(2):
        row = jnp.broadcast_to(pos_row(pos, 2 * h, 2), (HALF, HALF))
        pos_rows[pl.ds(h * HALF, HALF), :] = row.T

    def pair(own, other, grad, matches, start, many, fresh=False):
        logits = scale * against(own[...], other[start : start + many, :]) + bias
        weight = jax.nn.sigmoid(logits) - matches(start, many).astype(F32)
        weights[:, :many] = weight.astype(BF16)
        for n, wide in COLUMNS:
            product = jnp.dot(
                weights[:, :many], other[start : start + many, n : n + wide],
                preferred_element_type=F32,
            )
            if fresh:
                grad[:, n : n + wide] = product
            else:
                grad[:, n : n + wide] += product

    def txt_matches(back):
        owner = lax.rem(blk - back + 32, 32)

        def matches(start, many):
            first = owner * ROWS + start
            column = first + lax.broadcasted_iota(jnp.int32, (ROWS, many), 1)
            mine = pos_rows[...]
            if many > HALF:
                mine = jnp.concatenate([mine, mine], axis=1)
            return mine == column

        return matches

    def img_matches(pos_ref):
        def matches(start, many):
            row = blk * ROWS + lax.broadcasted_iota(jnp.int32, (ROWS, many), 0)
            mine = pos_row(pos_ref, start // 128, many // 128)
            return jnp.broadcast_to(mine, (ROWS, many)) == row

        return matches

    def pair_txt(other, back, start, many, fresh=False):
        pair(img_own, other, img_grad, txt_matches(back), start, many, fresh)

    def pair_img(other, pos_ref, start, many, fresh=False):
        pair(txt_own, other, txt_grad, img_matches(pos_ref), start, many, fresh)

    pair_txt(txt_own, 0, 0, ROWS, fresh=True)
    pair_img(img_own, pos, 0, ROWS, fresh=True)

    pos_ahead.wait_recv()

    @pl.when(c == 0)
    def _():
        pos_aside(pos_dir).start()

    pos_aside(pos).wait_recv()

    def side_txt(start, many):
        for index in range(start // MSG, (start + many) // MSG):
            txt_aside(txt_own, index).wait_recv()
        pair_txt(txt_side, 1, start, many)

    def side_img(start, many):
        for index in range(start // MSG, (start + many) // MSG):
            img_aside(img_own, index).wait_recv()
        pair_img(img_side, pos_side, start, many)

    @pl.when(c == 1)
    def _():
        side_txt(0, ROWS)

    @pl.when(c == 0)
    def _():
        side_img(0, ROWS)

    for h in range(2):
        for index in range(h * HALF // MSG, (h + 1) * HALF // MSG):
            txt_direct(index).wait_recv()

            @pl.when(c == 1)
            def _():
                txt_aside(txt_dir, index).start()

        if h == 1:
            for index in range(NMSG):
                txt_direct(index).wait_send()
            for d in range(1, 4):
                pl.semaphore_signal(
                    turn_sem, inc=1, device_id=device(x, y_peer(d), z, c), device_id_type=MESH
                )
            pl.semaphore_signal(turn_sem, inc=1, device_id=sibling, device_id_type=MESH)
            pl.semaphore_wait(turn_sem, 4)
            for index in range(NMSG):
                img_direct(index).start()
        pair_txt(txt_dir, 2, h * HALF, HALF)

        @pl.when(c == 0)
        def _():
            side_txt(h * HALF, HALF)

    def finish(grad, exact, inv, delta):
        def rows(i, _):
            for j in range(4):
                at = pl.ds(pl.multiple_of(i * 128 + j * 32, 32), 32)
                value = scale * grad[at, :]
                unit = exact[at, :]
                along = jnp.sum(unit * value, axis=-1, keepdims=True)
                delta[at, :] = (inv[at, :] * (value - unit * along)).astype(BF16)
            return 0

        lax.fori_loop(0, ROWS // 128, rows, 0)

    def waiter(ref, sem):
        return pltpu.make_async_copy(ref, ref, sem)

    class Chunk:
        def __init__(self, u, ch):
            self.u, self.ch = u, ch
            first, count = CHUNKS[ch]
            self.t = pl.ds(first, count)
            self.first, self.count = first, count
            order = ORDERS[u][ch]
            self.order = order
            self.is_root, self.own_target = is_root[order], own_target[order]
            self.near = x if order == "x" else y
            self.far = window[order]

        def near_peer(self, d):
            if self.order == "x":
                return x_peer(d), device(x_peer(d), y, z, c)
            return y_peer(d), device(x, y_peer(d), z, c)

        def far_peer(self, d):
            if self.order == "x":
                return y_peer(d), device(x, y_peer(d), z, c)
            return x_peer(d), device(x_peer(d), y, z, c)

        def sem(self, stage):
            return rs_send.at[self.u, self.ch, stage], rs_recv.at[self.u, self.ch, stage]

        def copy(self, stage, src, dst, target):
            send, recv = self.sem(stage)
            pltpu.make_async_remote_copy(
                src, dst, send, recv, device_id=target, device_id_type=MESH
            ).start()

        def make(self, feat, delta):
            columns = pl.ds(self.first * 128, self.count * 128)
            value = lax.dot_general(
                feat[...], delta[:, columns], (((0,), (0,)), ((), ())),
                preferred_element_type=F32,
            ).astype(BF16)
            for i in range(self.count):
                part[self.u, self.first + i] = value[:, i * 128 : (i + 1) * 128]
            other = pl.ds(pl.multiple_of(576 * (1 - c), 576), 576)
            self.copy(0, part.at[self.u, self.t, other], r1.at[self.u, self.t], sibling)

        def add_core(self):
            u, t = self.u, self.t
            send, recv = self.sem(0)
            waiter(r1.at[u, t], recv).wait()

            def step(i, _):
                tile = self.first + i
                mine = pl.ds(pl.multiple_of(576 * c, 576), 576)
                r1[u, tile] = (
                    part[u, tile, mine, :].astype(F32) + r1[u, tile].astype(F32)
                ).astype(BF16)
                return 0

            lax.fori_loop(0, self.count, step, 0)
            for d in range(1, 4):
                place, target = self.near_peer(d)
                rows = pl.ds(pl.multiple_of(ZROWS * place, ZROWS), ZROWS)
                self.copy(1, r1.at[u, t, rows], ra.at[u, d - 1, t], target)

        def add_near(self):
            u, t = self.u, self.t
            waiter(ra.at[u, :, t], self.sem(1)[1]).wait()

            def step(i, _):
                tile = self.first + i
                rows = pl.ds(pl.multiple_of(ZROWS * self.near, ZROWS), ZROWS)
                total = r1[u, tile, rows, :].astype(F32)
                for d in range(3):
                    total = total + ra[u, d, tile].astype(F32)
                q2[u, tile] = total.astype(BF16)
                return 0

            lax.fori_loop(0, self.count, step, 0)
            for d in range(1, 4):
                place, target = self.far_peer(d)
                rows = pl.ds(pl.multiple_of(32 * place, 32), WIN)
                self.copy(2, q2.at[u, t, rows], rb.at[u, d - 1, t], target)

        def add_far(self):
            u, t = self.u, self.t
            waiter(rb.at[u, :, t], self.sem(2)[1]).wait()

            def step(i, _):
                tile = self.first + i
                rows = pl.ds(pl.multiple_of(32 * self.far, 32), WIN)
                total = q2[u, tile, rows, :].astype(F32)
                for d in range(3):
                    total = total + rb[u, d, tile].astype(F32)
                q3[u, tile] = total.astype(BF16)
                return 0

            lax.fori_loop(0, self.count, step, 0)

            @pl.when(jnp.logical_not(self.is_root))
            def _():
                far_z = root_z[self.order]
                slot = lax.rem(z - far_z + 8, 8) - 1
                self.copy(3, q3.at[u, t], rz.at[u, slot, t], device(x, y, far_z, c))

        def targets(self):
            for dx in range(4):
                for dy in range(2):
                    far_y = 2 * (self.far // 2) + lax.rem(y_lo + dy, 2)
                    yield (dx, dy), device(x_peer(dx), far_y, z, lax.rem(self.far, 2))

        def add_z(self):
            u, t = self.u, self.t

            @pl.when(self.is_root)
            def _():
                waiter(rz.at[u, :, t], self.sem(3)[1]).wait()

                def step(i, _):
                    tile = self.first + i
                    total = q3[u, tile].astype(F32)
                    for d in range(7):
                        total = total + rz[u, d, tile].astype(F32)
                    q4[u, tile] = total.astype(BF16)
                    return 0

                lax.fori_loop(0, self.count, step, 0)
                for where, target in self.targets():
                    if where != (0, 0):
                        self.copy(4, q4.at[u, t], fin.at[u, t], target)
                    else:

                        @pl.when(self.own_target)
                        def _():
                            pltpu.make_async_copy(
                                q4.at[u, t], fin.at[u, t], self.sem(4)[1]
                            ).start()

                        @pl.when(jnp.logical_not(self.own_target))
                        def _():
                            pltpu.make_async_remote_copy(
                                q4.at[u, t], fin.at[u, t],
                                self_send.at[u, self.ch], self.sem(4)[1],
                                device_id=target, device_id_type=MESH,
                            ).start()

        def collect(self, out):
            u = self.u
            waiter(fin.at[u, self.t], self.sem(4)[1]).wait()
            for q in range(4):

                @pl.when(quarter == q)
                def _():
                    for i in range(self.count):
                        tile = self.first + i
                        out[:, tile * 128 : (tile + 1) * 128] = fin[u, tile].astype(F32)[
                            4 * q : 4 * q + OUT_ROWS
                        ]

        def drain(self):
            u, t = self.u, self.t
            waiter(r1.at[u, t], self.sem(0)[0]).wait()
            waiter(ra.at[u, :, t], self.sem(1)[0]).wait()
            waiter(rb.at[u, :, t], self.sem(2)[0]).wait()

            @pl.when(jnp.logical_not(self.is_root))
            def _():
                waiter(q3.at[u, t], self.sem(3)[0]).wait()

            @pl.when(self.is_root)
            def _():
                waiter(rz.at[u, :, t], self.sem(4)[0]).wait()

                @pl.when(jnp.logical_not(self.own_target))
                def _():
                    waiter(q4.at[u, t], self_send.at[u, self.ch]).wait()

    img_chunks = [Chunk(0, ch) for ch in range(NCH)]
    txt_chunks = [Chunk(1, ch) for ch in range(NCH)]

    def back(delta, proj, staged, out, index):
        for n, wide in COLUMNS:
            staged[:, n : n + wide] = against(delta[...], proj[n : n + wide, :]).astype(BF16)
        copy = pltpu.make_async_copy(staged, out, store_sem.at[index])
        copy.start()
        return copy

    finish(img_grad, img_exact, img_inv, img_delta)
    for chunk in img_chunks:
        chunk.make(img_feat, img_delta)
    for chunk in img_chunks:
        chunk.add_core()
    img_store = back(img_delta, img_proj, img_back, img_back_hbm, 0)

    for h in range(2):
        for index in range(h * HALF // MSG, (h + 1) * HALF // MSG):
            img_direct(index).wait_recv()

            @pl.when(c == 0)
            def _():
                img_aside(img_dir, index).start()

        pair_img(img_dir, pos_dir, h * HALF, HALF)

        @pl.when(c == 1)
        def _():
            side_img(h * HALF, HALF)

        if h == 0:
            for chunk in img_chunks:
                chunk.add_near()

    finish(txt_grad, txt_exact, txt_inv, txt_delta)
    for chunk in txt_chunks:
        chunk.make(txt_feat, txt_delta)
    for chunk in img_chunks:
        chunk.add_far()
    for chunk in txt_chunks:
        chunk.add_core()
    txt_store = back(txt_delta, txt_proj, txt_back, txt_back_hbm, 1)
    for chunk in img_chunks:
        chunk.add_z()
    for chunk in txt_chunks:
        chunk.add_near()
    for chunk in txt_chunks:
        chunk.add_far()
    for chunk in img_chunks:
        chunk.collect(img_out)
    for chunk in txt_chunks:
        chunk.add_z()
    for chunk in txt_chunks:
        chunk.collect(txt_out)

    img_store.wait()
    txt_store.wait()
    for chunk in img_chunks + txt_chunks:
        chunk.drain()
    for index in range(NMSG):
        img_direct(index).wait_send()
        txt_aside(txt_own, index).wait_send()
        img_aside(img_own, index).wait_send()
    pos_ahead.wait_send()
    pos_aside(pos).wait_send()


def deliver(*refs):
    sources, targets, held, load_sem, store_sem = refs[:4], refs[4:8], refs[8:12], refs[12], refs[13]
    loads = [
        pltpu.make_async_copy(sources[i], held[i], load_sem.at[i]) for i in range(4)
    ]
    stores = [
        pltpu.make_async_copy(held[i], targets[i], store_sem.at[i]) for i in range(4)
    ]
    for load in loads:
        load.start()
    for load, store in zip(loads, stores):
        load.wait()
        store.start()
    for store in stores:
        store.wait()


def per_device(img_feat, txt_feat, img_proj, txt_proj, pos_index, logit_scale, logit_bias):
    pos = pos_index.reshape(4, 128)
    anywhere = pl.BlockSpec(memory_space=pl.ANY)
    scalar = pl.BlockSpec(memory_space=pltpu.SMEM)
    vmem = pl.BlockSpec(memory_space=pltpu.VMEM)
    block16 = pltpu.VMEM((ROWS, WIDTH), BF16)
    block32 = pltpu.VMEM((ROWS, WIDTH), F32)
    square = pltpu.VMEM((WIDTH, WIDTH), BF16)
    places = pltpu.VMEM((4, 128), jnp.int32)
    dma = pltpu.SemaphoreType.DMA
    results = pl.pallas_call(
        kernel,
        name="pairwise",
        out_shape=(
            jax.ShapeDtypeStruct((ROWS, WIDTH), BF16),
            jax.ShapeDtypeStruct((ROWS, WIDTH), BF16),
            jax.ShapeDtypeStruct((OUT_ROWS, WIDTH), F32),
            jax.ShapeDtypeStruct((OUT_ROWS, WIDTH), F32),
        ),
        in_specs=[anywhere] * 5 + [scalar] * 2,
        out_specs=(anywhere, anywhere, vmem, vmem),
        scratch_shapes=[
            block16, block16, square, square, places,
            block16, block16, block16, block16, block16, block16, places, places,
            pltpu.VMEM((ROWS, HALF), jnp.int32),
            block32, block32, pltpu.VMEM((ROWS, 1), F32), pltpu.VMEM((ROWS, 1), F32),
            block32, block32, pltpu.VMEM((ROWS, ROWS), BF16),
            block16, block16, block16, block16,
            pltpu.VMEM((2, TILES, WIDTH, 128), BF16),
            pltpu.VMEM((2, TILES, WIDTH // 2, 128), BF16),
            pltpu.VMEM((2, 3, TILES, ZROWS, 128), BF16),
            pltpu.VMEM((2, TILES, ZROWS, 128), BF16),
            pltpu.VMEM((2, 3, TILES, WIN, 128), BF16),
            pltpu.VMEM((2, TILES, WIN, 128), BF16),
            pltpu.VMEM((2, 7, TILES, WIN, 128), BF16),
            pltpu.VMEM((2, TILES, WIN, 128), BF16),
            pltpu.VMEM((2, TILES, WIN, 128), BF16),
            dma((5,)), dma((2,)),
            dma((NMSG,)), dma((NMSG,)), dma((NMSG,)), dma((NMSG,)),
            dma((NMSG,)), dma((NMSG,)), dma((NMSG,)), dma((NMSG,)),
            dma((2,)), dma((2,)),
            dma((2, NCH, 5)), dma((2, NCH, 5)), dma((2, NCH)),
            pltpu.SemaphoreType.REGULAR,
        ],
        compiler_params=pltpu.CompilerParams(
            collective_id=0, has_side_effects=True, vmem_limit_bytes=62 * 1024 * 1024
        ),
        cost_estimate=pl.CostEstimate(
            flops=15_000_000_000, bytes_accessed=12_000_000, transcendentals=1_500_000
        ),
    )(img_feat, txt_feat, img_proj, txt_proj, pos, logit_scale, logit_bias)
    return pl.pallas_call(
        deliver,
        name="deliver",
        out_shape=tuple(jax.ShapeDtypeStruct(item.shape, item.dtype) for item in results),
        in_specs=[anywhere] * 4,
        out_specs=(anywhere,) * 4,
        scratch_shapes=[pltpu.VMEM(item.shape, item.dtype) for item in results]
        + [dma((4,)), dma((4,))],
    )(*results)


def solution(mesh):
    both = P(("group", "blk"), None)
    in_specs = (both, both, P(), P(), P(("group", "blk")), P(), P())
    out_specs = (both, both, P("blk", None), P("blk", None))
    return jax.shard_map(
        per_device, mesh=mesh, in_specs=in_specs, out_specs=out_specs, check_vma=False
    )
```

time: 122 us -> 108 us (0.89); the launches traced: 122 us -> 106 us
  Pallas kernels: 113 us -> 104 us
  local copies, waits for them, and re-layouts: 6.21 us -> 0 us
    pallas_call x1, Pallas kernels: 113 us -> 101 us  [per_device(): pl.pallas_call(kernel, name='pairwise', out_shape=(jax.ShapeDtypeStruct((...]
    unnamed x10 -> x0, local copies, waits for them, and re-layouts: 4.91 us -> none
    pallas_call x0 -> x1, Pallas kernels: none -> 2.85 us  [per_device(): pl.pallas_call(deliver, name='deliver', out_shape=tuple((jax.ShapeDtypeSt...]
where the time goes in v2:
time: 108 us; the launch traced here: 106 us
  Pallas kernels  104 us (96%)
  between operations  2.11 us (2%)
    pallas_call x1, Pallas kernels, per_device(): pl.pallas_call(kernel, name='pairwise', out_shape=(jax.ShapeDtypeStruct((...  101 us
    pallas_call x1, Pallas kernels, per_device(): pl.pallas_call(deliver, name='deliver', out_shape=tuple((jax.ShapeDtypeSt...  2.85 us

profile of v2, /device:TPU:1, one launch (start us, length us, event | category | flops | bytes accessed | tf_op | source)
XLA Modules:
  0.0 105.8 jit_solution(12018286895739325606)
XLA Ops:
  1.9 100.8 %pairwise.1 = (bf16[512,1152]{1,0:T(8,128)(2,1)}, bf16[512,1152]{1,0:T(8,128)(2,1)}, f32[36,1152]{1,0:T(8,128)}, f32[36,1152]{1,0:T(8,128)}) custom-call(bf16[512,1152]{1,0:T(8,128)(2,1)} %img_feat_hbm.1, bf16[512,1152]{1,0:T(8,128)(2,1)} %txt_feat_hbm.1, bf16[1152,1152]{1,0:T(8,128)(2,1)} %img_proj_hbm.1, bf16[1152,1152]{1,0:T(8,128)(2,1)} %txt_proj_hbm.1, ...), custom_call_target="tpu_custom_call" | custom-call | flops 15000000512 | bytes 12000000 | tf_op jit(solution)/shard_map/pairwise/pallas_call | solution.py:577
  102.8 2.9 %deliver.1 = (bf16[512,1152]{1,0:T(8,128)(2,1)}, bf16[512,1152]{1,0:T(8,128)(2,1)}, f32[36,1152]{1,0:T(8,128)}, f32[36,1152]{1,0:T(8,128)}) custom-call(bf16[512,1152]{1,0:T(8,128)(2,1)} %get-tuple-element.8.refs_0_, bf16[512,1152]{1,0:T(8,128)(2,1)} %get-tuple-element.9.refs_1_, f32[36,1152]{1,0:T(8,128)} %get-tuple-element.10.refs_2_, ...), custom_call_target="tpu_custom_call" | custom-call | tf_op jit(solution)/shard_map/deliver/pallas_call | solution.py:618

commit v3 on v2

--- a/solution.py
+++ b/solution.py
@@ -18,7 +18,7 @@
 PER_STEP = STEP // MSG
 TILES = WIDTH // 128
 CHUNKS = ((0, 2), (2, 2), (4, 2), (6, 2), (8, 1))
-ORDERS = ("xxxxx", "xyxyx")
+ORDERS = ("x", "m")
 COLUMNS = tuple((n, min(256, WIDTH - n)) for n in range(0, WIDTH, 256))
 NCH = len(CHUNKS)
 ZROWS = 144
@@ -82,7 +82,7 @@
         load(3, img_feat_hbm, img_feat),
         load(4, pos_hbm, pos),
     ]
-    for item in loads:
+    for item in loads[:2]:
         item.start()
 
     barrier = pltpu.get_barrier_semaphore()
@@ -153,6 +153,8 @@
 
     loads[0].wait()
     loads[1].wait()
+    for item in loads[2:]:
+        item.start()
     for step in range(ROWS // STEP):
         embed(txt_feat, txt_proj, txt_exact, txt_own, txt_inv, step * STEP)
         if step == 0:
@@ -274,14 +276,15 @@
             def _():
                 txt_aside(txt_dir, index).start()
 
+            txt_direct(index).wait_send()
+            if index == NMSG - 2:
+                for d in range(1, 4):
+                    pl.semaphore_signal(
+                        turn_sem, inc=1, device_id=device(x, y_peer(d), z, c), device_id_type=MESH
+                    )
+                pl.semaphore_signal(turn_sem, inc=1, device_id=sibling, device_id_type=MESH)
+
         if h == 1:
-            for index in range(NMSG):
-                txt_direct(index).wait_send()
-            for d in range(1, 4):
-                pl.semaphore_signal(
-                    turn_sem, inc=1, device_id=device(x, y_peer(d), z, c), device_id_type=MESH
-                )
-            pl.semaphore_signal(turn_sem, inc=1, device_id=sibling, device_id_type=MESH)
             pl.semaphore_wait(turn_sem, 4)
             for index in range(NMSG):
                 img_direct(index).start()
@@ -312,21 +315,25 @@
             first, count = CHUNKS[ch]
             self.t = pl.ds(first, count)
             self.first, self.count = first, count
-            order = ORDERS[u][ch]
-            self.order = order
-            self.is_root, self.own_target = is_root[order], own_target[order]
-            self.near = x if order == "x" else y
-            self.far = window[order]
+            order = ORDERS[u]
+            self.along_x = (c == 0) if order == "m" else (c >= 0)
+            self.is_root = self.choose(is_root["x"], is_root["y"])
+            self.own_target = self.choose(own_target["x"], own_target["y"])
+            self.root_z = self.choose(root_z["x"], root_z["y"])
+            self.near, self.far = self.choose(x, y), self.choose(y, x)
+
+        def choose(self, if_x, if_y):
+            if if_x.dtype == jnp.bool_:
+                return (self.along_x & if_x) | (jnp.logical_not(self.along_x) & if_y)
+            return jnp.where(self.along_x, if_x, if_y)
 
         def near_peer(self, d):
-            if self.order == "x":
-                return x_peer(d), device(x_peer(d), y, z, c)
-            return y_peer(d), device(x, y_peer(d), z, c)
+            target = device(self.choose(x_peer(d), x), self.choose(y, y_peer(d)), z, c)
+            return self.choose(x_peer(d), y_peer(d)), target
 
         def far_peer(self, d):
-            if self.order == "x":
-                return y_peer(d), device(x, y_peer(d), z, c)
-            return x_peer(d), device(x_peer(d), y, z, c)
+            target = device(self.choose(x, x_peer(d)), self.choose(y_peer(d), y), z, c)
+            return self.choose(y_peer(d), x_peer(d)), target
 
         def sem(self, stage):
             return rs_send.at[self.u, self.ch, stage], rs_recv.at[self.u, self.ch, stage]
@@ -403,7 +410,7 @@
 
             @pl.when(jnp.logical_not(self.is_root))
             def _():
-                far_z = root_z[self.order]
+                far_z = self.root_z
                 slot = lax.rem(z - far_z + 8, 8) - 1
                 self.copy(3, q3.at[u, t], rz.at[u, slot, t], device(x, y, far_z, c))
 
@@ -517,16 +524,21 @@
     finish(txt_grad, txt_exact, txt_inv, txt_delta)
     for chunk in txt_chunks:
         chunk.make(txt_feat, txt_delta)
+    for chunk in txt_chunks:
+        chunk.add_core()
     for chunk in img_chunks:
         chunk.add_far()
-    for chunk in txt_chunks:
-        chunk.add_core()
     txt_store = back(txt_delta, txt_proj, txt_back, txt_back_hbm, 1)
+    txt_chunks[0].add_near()
     for chunk in img_chunks:
         chunk.add_z()
-    for chunk in txt_chunks:
-        chunk.add_near()
-    for chunk in txt_chunks:
+    txt_chunks[1].add_near()
+    txt_chunks[2].add_near()
+    txt_chunks[0].add_far()
+    txt_chunks[3].add_near()
+    txt_chunks[1].add_far()
+    txt_chunks[4].add_near()
+    for chunk in txt_chunks[2:]:
         chunk.add_far()
     for chunk in img_chunks:
         chunk.collect(img_out)
@@ -549,12 +561,13 @@
 
 def deliver(*refs):
     sources, targets, held, load_sem, store_sem = refs[:4], refs[4:8], refs[8:12], refs[12], refs[13]
-    loads = [
-        pltpu.make_async_copy(sources[i], held[i], load_sem.at[i]) for i in range(4)
-    ]
-    stores = [
-        pltpu.make_async_copy(held[i], targets[i], store_sem.at[i]) for i in range(4)
-    ]
+    places = [(i, pl.ds(row, 128)) for i in range(2) for row in range(0, ROWS, 128)]
+    places += [(i, slice(None)) for i in (2, 3)]
+    loads, stores = [], []
+    for n, (i, at) in enumerate(places):
+        here = held[i].at[at]
+        loads.append(pltpu.make_async_copy(sources[i].at[at], here, load_sem.at[n]))
+        stores.append(pltpu.make_async_copy(here, targets[i].at[at], store_sem.at[n]))
     for load in loads:
         load.start()
     for load, store in zip(loads, stores):
@@ -622,7 +635,7 @@
         in_specs=[anywhere] * 4,
         out_specs=(anywhere,) * 4,
         scratch_shapes=[pltpu.VMEM(item.shape, item.dtype) for item in results]
-        + [dma((4,)), dma((4,))],
+        + [dma((10,)), dma((10,))],
     )(*results)
 
 

time: 108 us -> 105 us (0.972); the launches traced: 106 us -> 104 us
  Pallas kernels: 104 us -> 102 us
    pallas_call x1, Pallas kernels: 101 us -> 99.6 us  [per_device(): pl.pallas_call(kernel, name='pairwise', out_shape=(jax.ShapeDtypeStruct((...]
where the time goes in v3:
time: 105 us; the launch traced here: 104 us
  Pallas kernels  102 us (97%)
  between operations  2.11 us (2%)
    pallas_call x1, Pallas kernels, per_device(): pl.pallas_call(kernel, name='pairwise', out_shape=(jax.ShapeDtypeStruct((...  99.6 us
    pallas_call x1, Pallas kernels, per_device(): pl.pallas_call(deliver, name='deliver', out_shape=tuple((jax.ShapeDtypeSt...  2.65 us

profile of v3, /device:TPU:1, one launch (start us, length us, event | category | flops | bytes accessed | tf_op | source)
XLA Modules:
  0.0 104.4 jit_solution(5542881619125076413)
XLA Ops:
  1.9 99.6 %pairwise.1 = (bf16[512,1152]{1,0:T(8,128)(2,1)}, bf16[512,1152]{1,0:T(8,128)(2,1)}, f32[36,1152]{1,0:T(8,128)}, f32[36,1152]{1,0:T(8,128)}) custom-call(bf16[512,1152]{1,0:T(8,128)(2,1)} %img_feat_hbm.1, bf16[512,1152]{1,0:T(8,128)(2,1)} %txt_feat_hbm.1, bf16[1152,1152]{1,0:T(8,128)(2,1)} %img_proj_hbm.1, bf16[1152,1152]{1,0:T(8,128)(2,1)} %txt_proj_hbm.1, ...), custom_call_target="tpu_custom_call" | custom-call | flops 15000000512 | bytes 12000000 | tf_op jit(solution)/shard_map/pairwise/pallas_call | solution.py:590
  101.5 2.6 %deliver.1 = (bf16[512,1152]{1,0:T(8,128)(2,1)}, bf16[512,1152]{1,0:T(8,128)(2,1)}, f32[36,1152]{1,0:T(8,128)}, f32[36,1152]{1,0:T(8,128)}) custom-call(bf16[512,1152]{1,0:T(8,128)(2,1)} %get-tuple-element.8.refs_0_, bf16[512,1152]{1,0:T(8,128)(2,1)} %get-tuple-element.9.refs_1_, f32[36,1152]{1,0:T(8,128)} %get-tuple-element.10.refs_2_, ...), custom_call_target="tpu_custom_call" | custom-call | tf_op jit(solution)/shard_map/deliver/pallas_call | solution.py:631

commit v4 on v3

--- a/solution.py
+++ b/solution.py
@@ -17,10 +17,10 @@
 NMSG = ROWS // MSG
 PER_STEP = STEP // MSG
 TILES = WIDTH // 128
-CHUNKS = ((0, 2), (2, 2), (4, 2), (6, 2), (8, 1))
+CHUNKS = (((0, 3), (3, 3), (6, 3)), ((0, 2), (2, 2), (4, 2), (6, 2), (8, 1)))
 ORDERS = ("x", "m")
 COLUMNS = tuple((n, min(256, WIDTH - n)) for n in range(0, WIDTH, 256))
-NCH = len(CHUNKS)
+NCH = 5
 ZROWS = 144
 WIN = 48
 OUT_ROWS = 36
@@ -38,7 +38,7 @@
     img_feat_hbm, txt_feat_hbm, img_proj_hbm, txt_proj_hbm, pos_hbm, scale_ref, bias_ref,
     img_back_hbm, txt_back_hbm, img_out, txt_out,
     img_feat, txt_feat, img_proj, txt_proj, pos,
-    img_own, txt_own, img_dir, txt_dir, img_side, txt_side, pos_dir, pos_side, pos_rows,
+    img_own, txt_own, img_in, txt_dir, txt_side, pos_dir, pos_side, pos_rows,
     img_exact, txt_exact, img_inv, txt_inv, img_grad, txt_grad, weights,
     img_delta, txt_delta, img_back, txt_back,
     part, r1, ra, q2, rb, q3, rz, q4, fin,
@@ -132,24 +132,24 @@
             own[at, :] = unit.astype(BF16)
             inv[at, :] = inverse
 
-    def message(src, dst, send, recv, index, target):
-        at = pl.ds(index * MSG, MSG)
+    def message(src, dst, send, recv, index, target, shift=0):
         return pltpu.make_async_remote_copy(
-            src.at[at], dst.at[at], send.at[index], recv.at[index],
-            device_id=target, device_id_type=MESH,
+            src.at[pl.ds(index * MSG, MSG)], dst.at[pl.ds(index * MSG + shift, MSG)],
+            send.at[index], recv.at[index], device_id=target, device_id_type=MESH,
         )
 
     def txt_direct(index):
         return message(txt_own, txt_dir, td_send, td_recv, index, following)
 
-    def img_direct(index):
-        return message(img_own, img_dir, id_send, id_recv, index, previous)
-
     def txt_aside(src, index):
         return message(src, txt_side, ts_send, ts_recv, index, sibling)
 
+    def img_direct(index):
+        return message(img_own, img_in, id_send, id_recv, index, previous)
+
     def img_aside(src, index):
-        return message(src, img_side, is_send, is_recv, index, sibling)
+        shift = 128 if index * MSG >= ROWS - STEP else ROWS + STEP
+        return message(src, img_in, is_send, is_recv, index, sibling, shift)
 
     loads[0].wait()
     loads[1].wait()
@@ -225,10 +225,10 @@
 
         return matches
 
-    def img_matches(pos_ref):
+    def img_matches(pieces):
         def matches(start, many):
             row = blk * ROWS + lax.broadcasted_iota(jnp.int32, (ROWS, many), 0)
-            mine = pos_row(pos_ref, start // 128, many // 128)
+            mine = jnp.concatenate([ref[i : i + 1, :] for ref, i in pieces], axis=1)
             return jnp.broadcast_to(mine, (ROWS, many)) == row
 
         return matches
@@ -236,11 +236,11 @@
     def pair_txt(other, back, start, many, fresh=False):
         pair(img_own, other, img_grad, txt_matches(back), start, many, fresh)
 
-    def pair_img(other, pos_ref, start, many, fresh=False):
-        pair(txt_own, other, txt_grad, img_matches(pos_ref), start, many, fresh)
+    def pair_img(other, pieces, start, fresh=False):
+        pair(txt_own, other, txt_grad, img_matches(pieces), start, 128 * len(pieces), fresh)
 
     pair_txt(txt_own, 0, 0, ROWS, fresh=True)
-    pair_img(img_own, pos, 0, ROWS, fresh=True)
+    pair_img(img_own, [(pos, i) for i in range(4)], 0, fresh=True)
 
     pos_ahead.wait_recv()
 
@@ -255,10 +255,9 @@
             txt_aside(txt_own, index).wait_recv()
         pair_txt(txt_side, 1, start, many)
 
-    def side_img(start, many):
-        for index in range(start // MSG, (start + many) // MSG):
+    def wait_aside(indices):
+        for index in indices:
             img_aside(img_own, index).wait_recv()
-        pair_img(img_side, pos_side, start, many)
 
     @pl.when(c == 1)
     def _():
@@ -266,7 +265,8 @@
 
     @pl.when(c == 0)
     def _():
-        side_img(0, ROWS)
+        wait_aside(range(NMSG))
+        pair_img(img_in, [(pos_side, i) for i in (3, 0, 1, 2)], ROWS)
 
     for h in range(2):
         for index in range(h * HALF // MSG, (h + 1) * HALF // MSG):
@@ -312,7 +312,7 @@
     class Chunk:
         def __init__(self, u, ch):
             self.u, self.ch = u, ch
-            first, count = CHUNKS[ch]
+            first, count = CHUNKS[u][ch]
             self.t = pl.ds(first, count)
             self.first, self.count = first, count
             order = ORDERS[u]
@@ -363,9 +363,7 @@
             def step(i, _):
                 tile = self.first + i
                 mine = pl.ds(pl.multiple_of(576 * c, 576), 576)
-                r1[u, tile] = (
-                    part[u, tile, mine, :].astype(F32) + r1[u, tile].astype(F32)
-                ).astype(BF16)
+                r1[u, tile] = part[u, tile, mine, :] + r1[u, tile]
                 return 0
 
             lax.fori_loop(0, self.count, step, 0)
@@ -486,8 +484,7 @@
                 def _():
                     waiter(q4.at[u, t], self_send.at[u, self.ch]).wait()
 
-    img_chunks = [Chunk(0, ch) for ch in range(NCH)]
-    txt_chunks = [Chunk(1, ch) for ch in range(NCH)]
+    img_chunks, txt_chunks = ([Chunk(u, ch) for ch in range(len(CHUNKS[u]))] for u in range(2))
 
     def back(delta, proj, staged, out, index):
         for n, wide in COLUMNS:
@@ -503,23 +500,42 @@
         chunk.add_core()
     img_store = back(img_delta, img_proj, img_back, img_back_hbm, 0)
 
-    for h in range(2):
-        for index in range(h * HALF // MSG, (h + 1) * HALF // MSG):
+    def receive(indices):
+        for index in indices:
             img_direct(index).wait_recv()
 
             @pl.when(c == 0)
             def _():
-                img_aside(img_dir, index).start()
-
-        pair_img(img_dir, pos_dir, h * HALF, HALF)
-
-        @pl.when(c == 1)
-        def _():
-            side_img(h * HALF, HALF)
-
-        if h == 0:
-            for chunk in img_chunks:
-                chunk.add_near()
+                img_aside(img_in, index).start()
+
+    receive(range(0, 4))
+    pair_img(img_in, [(pos_dir, 0), (pos_dir, 1)], 0)
+
+    @pl.when(c == 1)
+    def _():
+        wait_aside(range(0, 4))
+        pair_img(img_in, [(pos_side, 0), (pos_side, 1)], ROWS + STEP)
+
+    for chunk in img_chunks:
+        chunk.add_near()
+    receive((4, 5))
+
+    @pl.when(c == 1)
+    def _():
+        pair_img(img_in, [(pos_dir, 2)], HALF)
+        wait_aside((4, 5))
+        pair_img(img_in, [(pos_side, 2)], 2 * ROWS - STEP)
+
+    receive((6, 7))
+
+    @pl.when(c == 0)
+    def _():
+        pair_img(img_in, [(pos_dir, 2), (pos_dir, 3)], HALF)
+
+    @pl.when(c == 1)
+    def _():
+        wait_aside((6, 7))
+        pair_img(img_in, [(pos_dir, 3), (pos_side, 3)], ROWS - STEP)
 
     finish(txt_grad, txt_exact, txt_inv, txt_delta)
     for chunk in txt_chunks:
@@ -600,7 +616,7 @@
         out_specs=(anywhere, anywhere, vmem, vmem),
         scratch_shapes=[
             block16, block16, square, square, places,
-            block16, block16, block16, block16, block16, block16, places, places,
+            block16, block16, pltpu.VMEM((2 * ROWS, WIDTH), BF16), block16, block16, places, places,
             pltpu.VMEM((ROWS, HALF), jnp.int32),
             block32, block32, pltpu.VMEM((ROWS, 1), F32), pltpu.VMEM((ROWS, 1), F32),
             block32, block32, pltpu.VMEM((ROWS, ROWS), BF16),

time: 105 us -> 104 us (level)
  no operation moved by 1% of the time
where the time goes in v4:
time: 104 us
  Pallas kernels  102 us (98%)
  between operations  2.11 us (2%)
    pallas_call x1, Pallas kernels, per_device(): pl.pallas_call(kernel, name='pairwise', out_shape=(jax.ShapeDtypeStruct((...  99.3 us
    pallas_call x1, Pallas kernels, per_device(): pl.pallas_call(deliver, name='deliver', out_shape=tuple((jax.ShapeDtypeSt...  2.65 us

profile of v4, /device:TPU:1, one launch (start us, length us, event | category | flops | bytes accessed | tf_op | source)
XLA Modules:
  0.0 104.1 jit_solution(16348432121659110795)
XLA Ops:
  1.9 99.3 %pairwise.1 = (bf16[512,1152]{1,0:T(8,128)(2,1)}, bf16[512,1152]{1,0:T(8,128)(2,1)}, f32[36,1152]{1,0:T(8,128)}, f32[36,1152]{1,0:T(8,128)}) custom-call(bf16[512,1152]{1,0:T(8,128)(2,1)} %img_feat_hbm.1, bf16[512,1152]{1,0:T(8,128)(2,1)} %txt_feat_hbm.1, bf16[1152,1152]{1,0:T(8,128)(2,1)} %img_proj_hbm.1, bf16[1152,1152]{1,0:T(8,128)(2,1)} %txt_proj_hbm.1, ...), custom_call_target="tpu_custom_call" | custom-call | flops 15000000512 | bytes 12000000 | tf_op jit(solution)/shard_map/pairwise/pallas_call | solution.py:606
  101.3 2.6 %deliver.1 = (bf16[512,1152]{1,0:T(8,128)(2,1)}, bf16[512,1152]{1,0:T(8,128)(2,1)}, f32[36,1152]{1,0:T(8,128)}, f32[36,1152]{1,0:T(8,128)}) custom-call(bf16[512,1152]{1,0:T(8,128)(2,1)} %get-tuple-element.8.refs_0_, bf16[512,1152]{1,0:T(8,128)(2,1)} %get-tuple-element.9.refs_1_, f32[36,1152]{1,0:T(8,128)} %get-tuple-element.10.refs_2_, ...), custom_call_target="tpu_custom_call" | custom-call | tf_op jit(solution)/shard_map/deliver/pallas_call | solution.py:647

commit v5 on v4

--- a/solution.py
+++ b/solution.py
@@ -17,7 +17,7 @@
 NMSG = ROWS // MSG
 PER_STEP = STEP // MSG
 TILES = WIDTH // 128
-CHUNKS = (((0, 3), (3, 3), (6, 3)), ((0, 2), (2, 2), (4, 2), (6, 2), (8, 1)))
+CHUNKS = (((0, 3), (3, 3), (6, 3)), ((0, 2), (2, 2), (4, 4), (8, 1)))
 ORDERS = ("x", "m")
 COLUMNS = tuple((n, min(256, WIDTH - n)) for n in range(0, WIDTH, 256))
 NCH = 5
@@ -549,11 +549,10 @@
     for chunk in img_chunks:
         chunk.add_z()
     txt_chunks[1].add_near()
+    txt_chunks[0].add_far()
     txt_chunks[2].add_near()
-    txt_chunks[0].add_far()
+    txt_chunks[1].add_far()
     txt_chunks[3].add_near()
-    txt_chunks[1].add_far()
-    txt_chunks[4].add_near()
     for chunk in txt_chunks[2:]:
         chunk.add_far()
     for chunk in img_chunks:

time: 104 us -> 106 us (1.019); the launches traced: 104 us -> 104 us
  no operation moved by 1% of the time
where the time goes in v5:
time: 106 us; the launch traced here: 104 us
  Pallas kernels  102 us (96%)
  between operations  2.11 us (2%)
    pallas_call x1, Pallas kernels, per_device(): pl.pallas_call(kernel, name='pairwise', out_shape=(jax.ShapeDtypeStruct((...  99.5 us
    pallas_call x1, Pallas kernels, per_device(): pl.pallas_call(deliver, name='deliver', out_shape=tuple((jax.ShapeDtypeSt...  2.65 us

profile of v5, /device:TPU:1, one launch (start us, length us, event | category | flops | bytes accessed | tf_op | source)
XLA Modules:
  0.0 104.2 jit_solution(8223759780787070006)
XLA Ops:
  1.9 99.5 %pairwise.1 = (bf16[512,1152]{1,0:T(8,128)(2,1)}, bf16[512,1152]{1,0:T(8,128)(2,1)}, f32[36,1152]{1,0:T(8,128)}, f32[36,1152]{1,0:T(8,128)}) custom-call(bf16[512,1152]{1,0:T(8,128)(2,1)} %img_feat_hbm.1, bf16[512,1152]{1,0:T(8,128)(2,1)} %txt_feat_hbm.1, bf16[1152,1152]{1,0:T(8,128)(2,1)} %img_proj_hbm.1, bf16[1152,1152]{1,0:T(8,128)(2,1)} %txt_proj_hbm.1, ...), custom_call_target="tpu_custom_call" | custom-call | flops 15000000512 | bytes 12000000 | tf_op jit(solution)/shard_map/pairwise/pallas_call | solution.py:605
  101.4 2.6 %deliver.1 = (bf16[512,1152]{1,0:T(8,128)(2,1)}, bf16[512,1152]{1,0:T(8,128)(2,1)}, f32[36,1152]{1,0:T(8,128)}, f32[36,1152]{1,0:T(8,128)}) custom-call(bf16[512,1152]{1,0:T(8,128)(2,1)} %get-tuple-element.8.refs_0_, bf16[512,1152]{1,0:T(8,128)(2,1)} %get-tuple-element.9.refs_1_, f32[36,1152]{1,0:T(8,128)} %get-tuple-element.10.refs_2_, ...), custom_call_target="tpu_custom_call" | custom-call | tf_op jit(solution)/shard_map/deliver/pallas_call | solution.py:646
